TPU v7x, 256 devices: a whole 4x4x8 slice. The times are simulated.
256 devices in a mesh: wide: 64 (over x, y, z_lo, core), narrow: 4 (over z_hi).
Axes of the slice: x: 4, y: 4, z: 8 (z_hi: 4, z_lo: 2; z = z_hi * 2 + z_lo), core: 2. Of those that a mesh axis runs over, the one named last changes fastest.
Arguments:
- raster: int32 [512, 8192], P('narrow', 'wide'), may hold values from 0 to 1
- transmission: bfloat16 [512, 8192], P('narrow', 'wide'), may hold values from 0.5 to 1.5
- kernels: float32 [8, 2, 64, 64], replicated, may hold values from -0.09375 to 0.09375
- kernel_weight: float32 [8], replicated, may hold values from 0.1 to 1
- library: bfloat16 [524288, 256], P(('wide', 'narrow')), may hold values from -40 to 40
- clip_tile: int32 [1024], replicated, may hold values from 0 to 255, as said below
- clip_corner: int32 [2, 1024], replicated, may hold values from 0 to 64
Outputs:
- aerial: float32 [512, 8192], P('narrow', 'wide')
- scores: float32 [1024], P(('wide', 'narrow'))
Inputs may be any that keep to these rules, and one draw needn't show every extreme that they name: `clip_tile`: each tile owns at most 16 clips, and some tile owns exactly 16.
All inputs are finite; a program needn't handle non-finite values.
Results may differ from a plain program's by a relative error of at most 0.0011.
Values may be sent and summed in bfloat16 or wider, within the bound.
A program may use at most 64 MiB of HBM per device.

v0:
```python
import math

import jax
import jax.numpy as jnp
from jax import lax
from jax.sharding import PartitionSpec as P

KSIZE = 64
CLIP = 64
KSIG = 16
CLIP_DEV = 4
CAP = 16


sharpness = 400.0
highest = lax.Precision.HIGHEST


def extended_2(block, sides, width):
    for axis, dim in sides:
        count = lax.axis_size(axis)
        forward = [(i, i + 1) for i in range(count - 1)]
        backward = [(target, source) for source, target in forward]
        low = lax.ppermute(
            lax.slice_in_dim(block, block.shape[dim] - width, None, axis=dim), axis, forward
        )
        high = lax.ppermute(lax.slice_in_dim(block, 0, width, axis=dim), axis, backward)
        block = jnp.concatenate([low, block, high], axis=dim)
    return block


def combined_all(value, axis, join):
    pieces = jax.tree.map(lambda part: lax.all_gather(part, axis), value)
    head = jax.tree.map(lambda part: part[0], pieces)
    tail = jax.tree.map(lambda part: part[1:], pieces)
    running, _ = lax.scan(lambda running, section: (join(running, section), None), head, tail)
    return running


def normalize(matrix):
    mean_square = jnp.mean(matrix * matrix, axis=1, keepdims=True)
    return (matrix / (KSIG * jnp.sqrt(mean_square + 1e-06))).astype(jnp.bfloat16)


def pair_product(formula, left_pair, right_pair):

    def single(left_operand, right_operand):
        return jnp.einsum(formula, left_operand, right_operand, precision=highest)

    real_part = single(left_pair[0], right_pair[0]) - single(left_pair[1], right_pair[1])
    imag_part = single(left_pair[0], right_pair[1]) + single(left_pair[1], right_pair[0])
    return (real_part, imag_part)


def shifted_basis(corner_rows, tile_size):
    freq_index = jnp.arange(KSIG, dtype=jnp.float32)[None, :, None]
    offset = jnp.arange(tile_size, dtype=jnp.int32)[None, None, :] - corner_rows[:, None, None]
    inside = (offset >= 0) & (offset < CLIP)
    weights = jnp.where(
        freq_index == 0, jnp.sqrt(jnp.float32(1.0 / CLIP)), jnp.sqrt(jnp.float32(2.0 / CLIP))
    )
    values = weights * jnp.cos(jnp.pi * (offset.astype(jnp.float32) + 0.5) * freq_index / CLIP)
    return jnp.where(inside, values, 0.0)


def library_parts(clip_units, lib_units):
    block_rows = min(512, lib_units.shape[0])
    blocks = lib_units.reshape(-1, block_rows, lib_units.shape[1])

    def absorb(running, lib_block):
        peak_old, total_old = running
        logits = sharpness * (
            jnp.einsum("cd,jd->cj", clip_units, lib_block, preferred_element_type=jnp.float32) - 1.0
        )
        peak_new = jnp.maximum(peak_old, jnp.max(logits, axis=1))
        total_new = total_old * jnp.exp(peak_old - peak_new) + jnp.sum(
            jnp.exp(logits - peak_new[:, None]), axis=1
        )
        return ((peak_new, total_new), None)

    rows_count = clip_units.shape[0]
    start_pair = (
        jnp.full((rows_count,), -1e30, jnp.float32),
        jnp.zeros((rows_count,), jnp.float32),
    )
    (peak_all, total_sum), unused = lax.scan(absorb, start_pair, blocks)
    return (peak_all, total_sum)


def blend_pairs(first_pair, second_pair):
    peak_both = jnp.maximum(first_pair[0], second_pair[0])
    total_both = first_pair[1] * jnp.exp(first_pair[0] - peak_both) + second_pair[1] * jnp.exp(
        second_pair[0] - peak_both
    )
    return (peak_both, total_both)


def per_device(raster, transmission, kernels, kernel_weight, library, clip_tile, clip_corner):
    tile_size = raster.shape[0]
    half_width = KSIZE // 2
    mask_values = raster.astype(jnp.bfloat16) * transmission
    extended = extended_2(mask_values, (("wide", 1), ("narrow", 0)), half_width).astype(jnp.float32)
    full_size = tile_size + 2 * half_width
    grid_index = jnp.arange(full_size, dtype=jnp.float32)
    phase_angle = (
        2.0 * math.pi / full_size * jnp.mod(grid_index[:, None] * grid_index[None, :], full_size)
    )
    fourier = (jnp.cos(phase_angle), -jnp.sin(phase_angle))
    inverse = (jnp.cos(phase_angle), jnp.sin(phase_angle))
    left_pair = (
        jnp.dot(fourier[0], extended, precision=highest),
        jnp.dot(fourier[1], extended, precision=highest),
    )
    spectrum = pair_product("ab,bc->ac", left_pair, fourier)
    kernel_taps = (kernels[:, 0], kernels[:, 1])
    narrow_cols = (inverse[0][:, :KSIZE], inverse[1][:, :KSIZE])
    sectioned = pair_product("ai,kij->kaj", narrow_cols, kernel_taps)
    transfer = pair_product("kaj,bj->kab", sectioned, narrow_cols)
    filtered = (
        spectrum[0][None] * transfer[0] - spectrum[1][None] * transfer[1],
        spectrum[0][None] * transfer[1] + spectrum[1][None] * transfer[0],
    )
    tile_rows = (inverse[0][:tile_size], inverse[1][:tile_size])
    partial_field = pair_product("xa,kab->kxb", tile_rows, filtered)
    tile_field = pair_product("kxb,yb->kxy", partial_field, tile_rows)
    inverse_scale = 1.0 / (full_size * full_size)
    energy = (tile_field[0] * inverse_scale) ** 2 + (tile_field[1] * inverse_scale) ** 2
    aerial = jnp.einsum("k,kxy->xy", kernel_weight, energy, precision=highest)
    cols_wide = lax.axis_size("wide")
    rows_narrow = lax.axis_size("narrow")
    own_tile = lax.axis_index("narrow") * cols_wide + lax.axis_index("wide")
    owned_clips = clip_tile == own_tile
    slot_rank = jnp.cumsum(owned_clips.astype(jnp.int32)) - 1
    slot_ids = jnp.arange(CAP, dtype=jnp.int32)
    select = (owned_clips[None, :] & (slot_rank[None, :] == slot_ids[:, None])).astype(jnp.int32)
    corner_rows = jnp.sum(select * clip_corner[0][None, :], axis=1)
    corner_cols = jnp.sum(select * clip_corner[1][None, :], axis=1)
    row_basis = shifted_basis(corner_rows, tile_size)
    col_basis = shifted_basis(corner_cols, tile_size)
    halfway = jnp.einsum("skx,xy->sky", row_basis, aerial, precision=highest)
    signature = jnp.einsum("sky,sly->skl", halfway, col_basis, precision=highest).reshape(
        CAP, KSIG * KSIG
    )
    signature = jnp.where(jnp.arange(KSIG * KSIG)[None, :] == 0, 0.0, signature)
    slot_units = normalize(signature)
    lib_units = normalize(library.astype(jnp.float32))
    clip_count = clip_tile.shape[0]
    earlier = jnp.arange(clip_count)[None, :] < jnp.arange(clip_count)[:, None]
    same_tile = clip_tile[None, :] == clip_tile[:, None]
    rank_all = jnp.sum((earlier & same_tile).astype(jnp.int32), axis=1)
    holder = clip_tile % cols_wide * rows_narrow + clip_tile // cols_wide
    position = holder * CAP + rank_all
    gathered = lax.all_gather(slot_units, ("wide", "narrow"), axis=0, tiled=True)
    peak_all, total_sum = library_parts(gathered[position], lib_units)
    flat_index = lax.axis_index("wide") * rows_narrow + lax.axis_index("narrow")
    peak_global, total_global = combined_all((peak_all, total_sum), ("wide", "narrow"), blend_pairs)
    peak_own = lax.dynamic_slice_in_dim(peak_global, flat_index * CLIP_DEV, CLIP_DEV)
    total_own = lax.dynamic_slice_in_dim(total_global, flat_index * CLIP_DEV, CLIP_DEV)
    scores = -(peak_own + jnp.log(total_own)) / sharpness
    return (aerial, scores)


def solution(mesh):
    placed = (
        P("narrow", "wide"),
        P("narrow", "wide"),
        P(),
        P(),
        P(("wide", "narrow"), None),
        P(),
        P(),
    )
    return jax.shard_map(
        per_device,
        mesh=mesh,
        in_specs=placed,
        out_specs=(P("narrow", "wide"), P(("wide", "narrow"))),
        check_vma=False,
    )
```

profile of v0, /device:TPU:32, one launch (start us, length us, event | category | flops | bytes accessed | tf_op | source)
XLA Modules:
  0.0 1866.7 jit_solution(9502491443086094996)
XLA Ops:
  8.8 1.9 collective-permute-start
  10.7 3.6 collective-permute-start.1
  22.6 1.4 fusion.18
  28.3 2.8 convolution_subtract_fusion
  31.1 1.5 convolution_add_fusion
  33.4 5.2 collective-permute-start.2
  38.6 1.8 collective-permute-start.3
  40.4 5.4 collective-permute-done.3
  45.8 1.9 fusion.58
  49.9 1.9 fusion.39
  54.1 3.1 fusion.25
  57.2 3.3 fusion.24
  60.5 3.1 fusion.10
  63.6 1.8 fusion.78
  65.4 1.8 fusion.79
  67.2 3.1 fusion.9
  70.3 1.8 fusion.15
  72.2 2.1 fusion.13
  80.0 695.4 %all-gather.6.cloned.1.call-done = bf16[4096,256]{1,0:T(8,128)(2,1)} async-done(((bf16[16,256]{1,0:T(8,128)(2,1)}), bf16[4096,256]{1,0:T(8,128)(2,1)}) %all-gather.6.cloned.1.call-update) | async-done | bytes 2097168 | tf_op jit(solution)/shard_map/all_gather | solution.py:153
  775.4 5.3 gather_fusion
  780.7 7.7 while.28
  789.8 526.4 %all-gather.8.cloned.1.call-done = f32[262144]{0:T(1024)} async-done(((f32[1024]{0:T(1024)}), f32[262144]{0:T(1024)}) %all-gather.8.cloned.1.call-update) | async-done | bytes 1048592 | tf_op jit(solution)/shard_map/all_gather | solution.py:33
  1317.6 526.0 %all-gather.10.cloned.1.call-done = f32[262144]{0:T(1024)} async-done(((f32[1024]{0:T(1024)}), f32[262144]{0:T(1024)}) %all-gather.10.cloned.1.call-update) | async-done | bytes 1048592 | tf_op jit(solution)/shard_map/all_gather | solution.py:33
  1845.5 13.8 while.27
  (615 shorter events, 44.2 us)
Async XLA Ops:
  7.2 67.1 %copy-start = (f32[8]{0:T(128)S(1)}, f32[8]{0:T(128)}, u32[]{:S(2)}) copy-start(f32[8]{0:T(128)} %param.14) | copy-start | bytes 100
  7.2 768.2 %all-gather.6.cloned.1.call-start = ((), (), s32[]{:S(2)}) async-start(), calls=%async_computation | async-start | bytes 2105344 | tf_op jit(solution)/shard_map/all_gather | solution.py:153
  8.1 7.1 copy-start.4
  8.8 23.8 %collective-permute-start = (bf16[128,32]{1,0:T(8,128)(2,1)}, bf16[128,32]{1,0:T(8,128)(2,1)}, u32[]{:S(2)}, u32[]{:S(2)}) collective-permute-start(bf16[128,32]{1,0:T(8,128)(2,1)} %get-tuple-element.152), channel_id=1, source_target_pairs={{0,4},{4,8},{8,12},{12,16},{16,20},{20,24},{24,28},{28,32},{32,36}... | collective-permute-start | bytes 24584 | tf_op jit(solution)/shard_map/ppermute | solution.py:24
  10.7 21.8 %collective-permute-start.1 = (bf16[128,32]{1,0:T(8,128)(2,1)}, bf16[128,32]{1,0:T(8,128)(2,1)}, u32[]{:S(2)}, u32[]{:S(2)}) collective-permute-start(bf16[128,32]{1,0:T(8,128)(2,1)} %get-tuple-element.153), channel_id=1, source_target_pairs={{4,0},{8,4},{12,8},{16,12},{20,16},{24,20},{28,24},{32,28},{36,32}... | collective-permute-start | bytes 24584 | tf_op jit(solution)/shard_map/ppermute | solution.py:27
  22.6 1.5 copy-start.9
  28.2 2.8 copy-start.1
  28.3 2.8 copy-start.2
  31.1 1.5 copy-start.5
  33.4 7.0 collective-permute-start.2
  38.6 7.2 collective-permute-start.3
  72.2 5.5 copy-start.3
  74.3 3.8 copy-start.10
  75.2 4.8 copy-start.7
  77.7 1238.6 %all-gather.8.cloned.1.call-start = ((), (), s32[]{:S(2)}) async-start(), calls=%async_computation.1 | async-start | bytes 1052672 | tf_op jit(solution)/shard_map/all_gather | solution.py:33
  788.5 0.6 copy-start.6
  788.5 0.7 copy-start.8
  789.1 1054.5 %all-gather.10.cloned.1.call-start = ((), (), s32[]{:S(2)}) async-start(), calls=%async_computation.2 | async-start | bytes 1052672 | tf_op jit(solution)/shard_map/all_gather | solution.py:33
  1316.3 1.2 slice-start
  1843.6 1.2 slice-start.2
  1844.8 0.7 slice-start.1
  1844.8 0.7 slice-start.3
Sparse Core Ops, SparseCore 0:
  77.8 697.5 all-gather.5
  789.2 527.0 all-gather.7
  1318.1 525.5 all-gather.9
where the time goes:
time: 1880 us; the launch traced here: 1870 us
  waiting for transfers between devices  1750 us (93%)
  matrix products  47.5 us (3%)
    all_gather x2, waiting for transfers between devices, combined_all(): pieces = jax.tree.map(lambda part: lax.all_gather(part, axis), value)  1050 us
    all_gather x1, waiting for transfers between devices, per_device(): lax.all_gather(slot_units, ('wide', 'narrow'), axis=0, tiled=True)  695 us
  transfers between devices with their start and end apart: 7, of which 4 were waited for; matrix products, arithmetic and copies ran while one was open for 1% of the time, Pallas kernels for 0%

commit v1 on v0

v1 whole, which is shorter than its diff:
```python
import math

import jax
import jax.numpy as jnp
from jax import lax
from jax.experimental import pallas as pl
from jax.experimental.pallas import tpu as pltpu
from jax.sharding import PartitionSpec as P

TILE = 128
TAPS = 64
HALF = 32
KSIG = 16
CAP = 16
SIGD = 256
FIELDS = 16
SHIFTS = 16
DEPTH = 5 * 1024
GROUPS = 16
OWN_IDS = 512
CLIPS = 1024
LIB_DEV = 2048
SHARP = 400.0
F32 = jnp.float32
BF16 = jnp.bfloat16
I32 = jnp.int32
MESH = pl.DeviceIdType.MESH
HIGHEST = lax.Precision.HIGHEST

PLANE = sorted(
    [(dx, dy) for dx in range(4) for dy in range(4) if dx or dy],
    key=lambda d: -(min(d[0], 4 - d[0]) + min(d[1], 4 - d[1])),
)
LINE = sorted(
    [(dz, dc) for dz in range(8) for dc in range(2) if dz or dc],
    key=lambda d: -(2 * min(d[0], 8 - d[0]) + d[1]),
)
RING = sorted(range(1, 8), key=lambda d: -min(d, 8 - d))
AROUND = [(dw, dn) for dw in (1, -1, 0) for dn in (1, -1, 0) if dw or dn]


def place():
    w = lax.axis_index("wide")
    n = lax.axis_index("narrow")
    return w, n


def plane_peer(w, n, d):
    g = w // 4
    x = (g // 4 + d[0]) % 4
    y = (g % 4 + d[1]) % 4
    return (x * 4 + y) * 4 + w % 4, n


def line_peer(w, n, d):
    z = (n * 2 + (w // 2) % 2 + d[0]) % 8
    c = (w % 2 + d[1]) % 2
    return (w // 4) * 4 + (z % 2) * 2 + c, z // 2


def around_peer(w, n, d):
    return (w + d[0] + 64) % 64, (n + d[1] + 4) % 4


def iota(shape, dim):
    return lax.broadcasted_iota(I32, shape, dim)


def dot(a, b, precision=None):
    return jnp.dot(a, b, preferred_element_type=F32, precision=precision)


def dot_nt(a, b, precision=None):
    return lax.dot_general(
        a, b, (((1,), (1,)), ((), ())), preferred_element_type=F32, precision=precision
    )


def wait_bytes(ref, sem):
    pltpu.make_async_copy(ref, ref, sem).wait()


def unit_rows(matrix):
    mean_square = jnp.mean(matrix * matrix, axis=1, keepdims=True)
    return (matrix / (KSIG * jnp.sqrt(mean_square + 1e-06))).astype(BF16)


def build_taps(kern_ref, raw_taps, perm, taps):
    for block in range(8):
        p = iota((128, 1024), 0) + block * 128
        q = iota((128, 1024), 1)
        hit = q == (p % 64) * 16 + p // 64
        perm[block * 128 : block * 128 + 128, :] = jnp.where(hit, 1.0, 0.0).astype(BF16)
    for i in range(0, TAPS, 2):
        pair = jnp.concatenate(
            [kern_ref[pl.ds(i, 16, stride=64), :], kern_ref[pl.ds(i + 1, 16, stride=64), :]],
            axis=1,
        )
        high = pair.astype(BF16)
        low = (pair - high.astype(F32)).astype(BF16)
        row = (i // 16) * 32
        lane = (i % 16) * 64
        raw_taps[row : row + 16, lane : lane + 128] = high
        raw_taps[row + 16 : row + 32, lane : lane + 128] = low
    raw_taps[...] = dot(raw_taps[...], perm[...]).astype(BF16)

    def shift(s, carry):
        inner = iota((32, 128), 1) % 16
        wrap = inner >= 16 - s
        row = pl.multiple_of(s * 16, 16)
        for v in range(8):
            lanes = slice(v * 128, v * 128 + 128)
            for ib in range(5):
                zero = jnp.zeros((32, 128), BF16)
                here = raw_taps[ib * 32 : ib * 32 + 32, lanes] if ib < 4 else zero
                if ib > 0:
                    last = pltpu.roll(raw_taps[ib * 32 - 32 : ib * 32, lanes], 112, 1)
                else:
                    last = zero
                moved = pltpu.roll(jnp.where(wrap, last, here), s, 1)
                to = slice(ib * 1024 + v * 128, ib * 1024 + v * 128 + 128)
                taps[pl.ds(row, 16), to] = moved[0:16]
                taps[pl.ds(row + 256, 16), to] = moved[16:32]
        return carry

    lax.fori_loop(0, SHIFTS, shift, 0)


def cosine(m):
    v = (64 - jnp.abs(m - 128)).astype(F32) * (math.pi / 128)
    s = v * v
    poly = 1.0 / 6227020800.0
    for c in (-1.0 / 39916800, 1.0 / 362880, -1.0 / 5040, 1.0 / 120, -1.0 / 6, 1.0):
        poly = poly * s + c
    return -(v * poly)


def shifted_basis(corner):
    spread = (iota((256, 16), 0) // 16 == iota((256, 16), 1)).astype(F32)
    corners = dot(spread, jnp.broadcast_to(corner, (16, 128))).astype(I32)
    k = iota((256, 128), 0) % 16
    offset = iota((256, 128), 1) - corners
    inside = (offset >= 0) & (offset < 64)
    weight = jnp.where(k == 0, math.sqrt(1.0 / 64), math.sqrt(2.0 / 64)).astype(F32)
    m = jnp.where(inside, ((2 * offset + 1) * k) % 256, 0)
    return jnp.where(inside, weight * cosine(m), 0.0)


def own_bases(w, n, tile_ref, corner_ref, row_basis, col_basis):
    owned = (tile_ref[...] == n * 64 + w).astype(F32)
    earlier = (iota((128, 128), 0) < iota((128, 128), 1)).astype(F32)
    before = dot(owned, earlier)
    base = jnp.zeros((1, 1), F32)
    slot = iota((16, 128), 0).astype(F32)
    rows = jnp.zeros((16, 128), F32)
    cols = jnp.zeros((16, 128), F32)
    for r in range(8):
        own = owned[r : r + 1]
        here = (own > 0) & (before[r : r + 1] + base == slot)
        part = slice(r * 128, r * 128 + 128)
        rows += jnp.where(here, corner_ref[0:1, part].astype(F32), 0.0)
        cols += jnp.where(here, corner_ref[1:2, part].astype(F32), 0.0)
        base += jnp.sum(own, axis=1, keepdims=True)
    row_basis[...] = shifted_basis(jnp.sum(rows, axis=1, keepdims=True))
    col_basis[...] = shifted_basis(jnp.sum(cols, axis=1, keepdims=True))


def build_select(w, tile_ref, select):
    core = w % 2
    q = iota((64, 256), 1)
    dev = q // 16
    slot_key = ((dev % 4) * 64 + (w // 4) * 4 + dev // 4) * 16 + q % 16
    for r in range(8):
        m = iota((64, 128), 0) + r * 64
        ids = (m // 16) * 32 + core * 16 + m % 16
        lane = iota((64, 128), 1)
        tiles = tile_ref[r : r + 1, :]
        mine = jnp.sum(
            jnp.where(ids == lane + r * 128, tiles.astype(F32), 0.0), axis=1, keepdims=True
        )
        rank = jnp.zeros((64, 128), F32)
        for b in range(r + 1):
            same = tile_ref[b : b + 1, :].astype(F32) == mine
            if b == r:
                same = same & (lane + r * 128 < ids)
            rank += jnp.where(same, 1.0, 0.0)
        key = (mine * 16.0 + jnp.sum(rank, axis=1, keepdims=True)).astype(I32)
        select[r * 64 : r * 64 + 64, :] = (key == slot_key).astype(F32).astype(BF16)


def shifted_copies(ext, spread):
    lane = iota((192, 128), 1)
    left = pltpu.roll(ext[0], HALF, 1)
    mid = pltpu.roll(ext[1], HALF, 1)
    right = pltpu.roll(ext[2], HALF, 1)
    low = jnp.where(lane < HALF, left, mid)
    high = jnp.where(lane < HALF, mid, right)
    for j in range(TAPS):
        moved = jnp.where(lane < j, high, low)
        if j:
            moved = pltpu.roll(moved, 128 - j, 1)
        for rb in range(12):
            block = moved[rb * 16 : rb * 16 + 16]
            if rb < 8:
                spread[rb * 1024 + j * 16 : rb * 1024 + j * 16 + 16, 0:128] = block
            if rb >= 4:
                at = (rb - 4) * 1024 + j * 16
                spread[at : at + 16, 128:256] = block


def kernel(
    raster_ref, trans_ref, kern_ref, weight_ref, lib_ref, tile_ref, corner_ref,
    aerial_ref, score_ref,
    mask, ext, raw_taps, perm, taps, spread, row_basis, col_basis, select,
    lib_raw, units, slots, parts, sums, clips, runs, ring_lse, plane_lse,
    halo_send, halo_recv, lib_sem, pair_send, pair_recv,
    line_send, line_recv, sum_send, sum_recv, all_send, all_recv,
    ring_send, ring_recv, plane_send, plane_recv,
):
    w, n = place()
    g = w // 4
    core = w % 2
    line_me = (w % 4) * 4 + n
    z_me = n * 2 + (w // 2) % 2
    around = [around_peer(w, n, d) for d in AROUND]
    line = [line_peer(w, n, d) for d in LINE]
    plane = [plane_peer(w, n, d) for d in PLANE]
    ring = [line_peer(w, n, (d, 0)) for d in RING]

    barrier = pltpu.get_barrier_semaphore()
    peers = around + line + plane
    for peer in peers:
        pl.semaphore_signal(barrier, inc=1, device_id=peer, device_id_type=MESH)
    lib_copy = pltpu.make_async_copy(lib_ref, lib_raw, lib_sem)
    lib_copy.start()
    mask[...] = (raster_ref[...].astype(F32) * trans_ref[...].astype(F32)).astype(BF16)
    ext[1, HALF : HALF + TILE, :] = mask[...]
    build_taps(kern_ref, raw_taps, perm, taps)
    pl.semaphore_wait(barrier, len(peers))

    def send(src, dst, ssem, rsem, peer):
        copy = pltpu.make_async_remote_copy(
            src_ref=src, dst_ref=dst, send_sem=ssem, recv_sem=rsem,
            device_id=peer, device_id_type=MESH,
        )
        copy.start()
        return copy

    halo = []
    for i, (dw, dn) in enumerate(AROUND):
        src = {0: mask, 1: mask.at[TILE - HALF : TILE], -1: mask.at[0:HALF]}[dn]
        to = {0: slice(HALF, HALF + TILE), 1: slice(0, HALF), -1: slice(HALF + TILE, 2 * HALF + TILE)}[dn]
        dst = ext.at[1 - dw, to]
        halo.append(send(src, dst, halo_send.at[i], halo_recv.at[i], around[i]))

    lib_copy.wait()

    def normal(i, carry):
        at = pl.ds(pl.multiple_of(i * 256, 256), 256)
        units[0, at, :] = unit_rows(lib_raw[at, :].astype(F32))
        return carry

    lax.fori_loop(0, LIB_DEV // 256, normal, 0)
    other = line_peer(w, n, (0, 1))
    pair = send(units.at[0], units.at[1], pair_send, pair_recv, other)
    own_bases(w, n, tile_ref, corner_ref, row_basis, col_basis)
    build_select(w, tile_ref, select)

    for copy in halo:
        copy.wait()
    zero_side = jnp.zeros((192, TILE), BF16)
    zero_rows = jnp.zeros((3, HALF, TILE), BF16)

    @pl.when(w == 0)
    def _():
        ext[0] = zero_side

    @pl.when(w == 63)
    def _():
        ext[2] = zero_side

    @pl.when(n == 0)
    def _():
        ext[:, 0:HALF, :] = zero_rows

    @pl.when(n == 3)
    def _():
        ext[:, HALF + TILE : 2 * HALF + TILE, :] = zero_rows

    shifted_copies(ext, spread)

    field_index = iota((16, 256), 0) // 2
    weight = jnp.zeros((16, 256), F32)
    for k in range(8):
        weight = jnp.where(field_index == k, weight_ref[k], weight)

    def rows(i, carry):
        window = spread[pl.ds(pl.multiple_of(i * 1024, 1024), DEPTH), :]
        both = dot(taps[...], window)
        field = both[0:256] + both[256:512]
        energy = (field * field).reshape(SHIFTS, FIELDS, 256) * weight[None]
        image = jnp.sum(energy, axis=1)
        at = pl.multiple_of(i * 16, 16)
        aerial_ref[pl.ds(at, 16), :] = image[:, 0:128]
        aerial_ref[pl.ds(at + 64, 16), :] = image[:, 128:256]
        return carry

    lax.fori_loop(0, 4, rows, 0)

    halfway = dot(row_basis[...], aerial_ref[...], HIGHEST)
    cross = dot_nt(halfway, col_basis[...], HIGHEST)
    row = iota((256, 256), 0)
    lane = iota((256, 256), 1)
    cross = jnp.where(row // 16 == lane // 16, cross, 0.0)
    fold = (row % 16 == lane % 16).astype(F32)
    wide = jnp.where(row % 16 == lane // 16, dot(cross, fold, HIGHEST), 0.0)
    signature = jnp.sum(wide.reshape(CAP, KSIG, SIGD), axis=1)
    signature = jnp.where(iota((CAP, SIGD), 1) == 0, 0.0, signature)
    slots[line_me] = unit_rows(signature)

    for peer in line:
        send(slots.at[line_me], slots.at[line_me], line_send, line_recv, peer)
    wait_bytes(slots.at[0:15], line_recv)
    picked = dot(select[...], slots[...].reshape(256, SIGD)).astype(BF16)
    parts[...] = picked.reshape(GROUPS, 32, SIGD)

    for i, d in enumerate(PLANE):
        gp = plane[i][0] // 4
        send(parts.at[gp], sums.at[g], sum_send, sum_recv, plane[i])
    sums[g] = parts[g]
    wait_bytes(sums.at[0:15], sum_recv)
    total = sums[0].astype(F32)
    for i in range(1, GROUPS):
        total += sums[i].astype(F32)
    clips[g] = total.astype(BF16)

    for peer in plane:
        send(clips.at[g], clips.at[g], all_send, all_recv, peer)
    pair.wait()
    wait_bytes(clips.at[0:15], all_recv)

    scale = SHARP * math.log2(math.e)
    for half in range(2):
        chosen = clips[half * 8 : half * 8 + 8].reshape(256, SIGD)
        runs[0] = jnp.full((8, 256), -4.0, F32)
        runs[1] = jnp.zeros((8, 256), F32)
        for source in range(2):

            def match(i, carry):
                block = units[source, pl.ds(pl.multiple_of(i * 512, 512), 512), :]
                near = dot_nt(block, chosen).reshape(64, 8, 256)
                old = runs[0]
                top = jnp.maximum(old, jnp.max(near, axis=0))
                gain = jnp.sum(jnp.exp2((near - top[None]) * scale), axis=0)
                runs[1] = runs[1] * jnp.exp2((old - top) * scale) + gain
                runs[0] = top
                return carry

            lax.fori_loop(0, LIB_DEV // 512, match, 0)
        tops = runs[0]
        top = jnp.max(tops, axis=0, keepdims=True)
        weighted = runs[1] * jnp.exp2((tops - top) * scale)
        amount = jnp.sum(weighted, axis=0, keepdims=True)
        ring_lse[z_me, :, half * 256 : half * 256 + 256] = (top - 1.0) * SHARP + jnp.log(amount)

    def joined(parts_ref, count):
        values = [parts_ref[i] for i in range(count)]
        top = values[0]
        for v in values[1:]:
            top = jnp.maximum(top, v)
        amount = jnp.exp(values[0] - top)
        for v in values[1:]:
            amount += jnp.exp(v - top)
        return top + jnp.log(amount)

    for peer in ring:
        send(ring_lse.at[z_me], ring_lse.at[z_me], ring_send, ring_recv, peer)
    wait_bytes(ring_lse.at[0:7], ring_recv)
    plane_lse[g] = joined(ring_lse, 8)
    for peer in plane:
        send(plane_lse.at[g], plane_lse.at[g], plane_send, plane_recv, peer)
    wait_bytes(plane_lse.at[0:15], plane_recv)
    score = joined(plane_lse, GROUPS) / (-SHARP)
    first = g * 32 + ((w // 2) % 2) * 16 + n * 4
    spot = iota((1, OWN_IDS), 1)
    for t in range(4):
        score_ref[t] = jnp.sum(jnp.where(spot == first + t, score, 0.0))

    wait_bytes(slots.at[0:15], line_send)
    wait_bytes(sums.at[0:15], sum_send)
    wait_bytes(clips.at[0:15], all_send)
    wait_bytes(ring_lse.at[0:7], ring_send)
    wait_bytes(plane_lse.at[0:15], plane_send)


def per_device(raster, transmission, kernels, kernel_weight, library, clip_tile, clip_corner):
    vmem = pl.BlockSpec(memory_space=pltpu.VMEM)
    smem = pl.BlockSpec(memory_space=pltpu.SMEM)
    dma = pltpu.SemaphoreType.DMA
    return pl.pallas_call(
        kernel,
        out_shape=(
            jax.ShapeDtypeStruct((TILE, TILE), F32),
            jax.ShapeDtypeStruct((4,), F32),
        ),
        in_specs=[vmem, vmem, vmem, smem, pl.BlockSpec(memory_space=pl.ANY), vmem, vmem],
        out_specs=(vmem, smem),
        scratch_shapes=[
            pltpu.VMEM((TILE, TILE), BF16),
            pltpu.VMEM((3, 192, TILE), BF16),
            pltpu.VMEM((128, 1024), BF16),
            pltpu.VMEM((1024, 1024), BF16),
            pltpu.VMEM((512, DEPTH), BF16),
            pltpu.VMEM((8 * 1024, 256), BF16),
            pltpu.VMEM((256, TILE), F32),
            pltpu.VMEM((256, TILE), F32),
            pltpu.VMEM((OWN_IDS, 256), BF16),
            pltpu.VMEM((LIB_DEV, SIGD), BF16),
            pltpu.VMEM((2, LIB_DEV, SIGD), BF16),
            pltpu.VMEM((16, CAP, SIGD), BF16),
            pltpu.VMEM((GROUPS, 32, SIGD), BF16),
            pltpu.VMEM((GROUPS, 32, SIGD), BF16),
            pltpu.VMEM((GROUPS, 32, SIGD), BF16),
            pltpu.VMEM((2, 8, 256), F32),
            pltpu.VMEM((8, 1, OWN_IDS), F32),
            pltpu.VMEM((GROUPS, 1, OWN_IDS), F32),
            dma((8,)), dma((8,)), dma, dma, dma,
            dma, dma, dma, dma, dma, dma, dma, dma, dma, dma,
        ],
        compiler_params=pltpu.CompilerParams(
            collective_id=0, has_side_effects=True, vmem_limit_bytes=56 * 1024 * 1024
        ),
    )(
        raster,
        transmission,
        kernels.reshape(FIELDS * TAPS, TAPS),
        kernel_weight,
        library,
        clip_tile.reshape(8, 128),
        clip_corner,
    )


def solution(mesh):
    placed = (
        P("narrow", "wide"),
        P("narrow", "wide"),
        P(),
        P(),
        P(("wide", "narrow"), None),
        P(),
        P(),
    )
    return jax.shard_map(
        per_device,
        mesh=mesh,
        in_specs=placed,
        out_specs=(P("narrow", "wide"), P(("wide", "narrow"))),
        check_vma=False,
    )
```

time: 1880 us -> 61.1 us (0.03)
  waiting for transfers between devices: 1750 us -> 0 us
  Pallas kernels: 0 us -> 58.2 us
  matrix products: 47.5 us -> 0 us
    all_gather x3 -> x0, waiting for transfers between devices: 1750 us -> none  [the longest x2 1050 us: combined_all(): pieces = jax.tree.map(lambda part: lax.all_gather(part, axis), value)]
    pallas_call x0 -> x1, Pallas kernels: none -> 58.2 us  [per_device(): pl.pallas_call(kernel, out_shape=(jax.ShapeDtypeStruct((TILE, TILE), F32)...]
    dot_general x25 -> x0, matrix products: 43.7 us -> none  [the longest x16 31.7 us: single(): return jnp.einsum(formula, left_operand, right_operand, precision=highest)]
  transfers between devices with their start and end apart: 7 -> 0, of which waited for: 4 -> 0; matrix products, arithmetic and copies ran while one was open for 1% -> 0% of each run, Pallas kernels for 0% -> 0%
where the time goes in v1:
time: 61.1 us; the launch traced here: 60.8 us
  Pallas kernels  58.2 us (95%)
  local copies, waits for them, and re-layouts  1.99 us (3%)
  between operations  0.65 us (1%)
    pallas_call x1, Pallas kernels, per_device(): pl.pallas_call(kernel, out_shape=(jax.ShapeDtypeStruct((TILE, TILE), F32)...  58.2 us
    unnamed x4, local copies, waits for them, and re-layouts  1.99 us

profile of v1, /device:TPU:32, one launch (start us, length us, event | category | flops | bytes accessed | tf_op | source)
XLA Modules:
  0.0 60.8 jit_solution(23960639198015834)
XLA Ops:
  0.6 58.2 %shard_map.86 = (f32[128,128]{1,0:T(8,128)}, f32[4]{0:T(128)}) custom-call(s32[128,128]{1,0:T(8,128)} %raster_ref.1, bf16[128,128]{1,0:T(8,128)(2,1)} %trans_ref.1, f32[1024,64]{1,0:T(8,128)} %bitcast.2, f32[8]{0:T(128)} %weight_ref.1, bf16[2048,256]{1,0:T(8,128)(2,1)} %lib_ref.1, s32[8,128]{1,0:T(8,128)} %bitcast.3, s32[2,1024]{1,0:T(2,128)} %corner_ref.1), custom_call_target="tpu_custom_call" | custom-call | tf_op jit(solution)/shard_map/pallas_call | solution.py:400
  58.8 0.0 copy-start
  58.8 1.5 %copy.11 = f32[128,128]{1,0:T(8,128)} copy(f32[128,128]{1,0:T(8,128)} %get-tuple-element.4) | data formatting | bytes 131072
  60.3 0.0 copy-done
  60.3 0.5 copy.12
Async XLA Ops:
  58.8 1.5 %copy-start = (f32[4]{0:T(128)S(1)}, f32[4]{0:T(128)}, u32[]{:S(2)}) copy-start(f32[4]{0:T(128)} %get-tuple-element.5) | copy-start | bytes 52

commit v2 on v1

--- a/solution.py
+++ b/solution.py
@@ -35,7 +35,10 @@
     [(dz, dc) for dz in range(8) for dc in range(2) if dz or dc],
     key=lambda d: -(2 * min(d[0], 8 - d[0]) + d[1]),
 )
-RING = sorted(range(1, 8), key=lambda d: -min(d, 8 - d))
+SAME_CORE = sorted(
+    [(dx, dy, dz) for dx in range(4) for dy in range(4) for dz in range(8) if dx or dy or dz],
+    key=lambda d: -(min(d[0], 4 - d[0]) + min(d[1], 4 - d[1]) + min(d[2], 8 - d[2])),
+)
 AROUND = [(dw, dn) for dw in (1, -1, 0) for dn in (1, -1, 0) if dw or dn]
 
 
@@ -56,6 +59,11 @@
     z = (n * 2 + (w // 2) % 2 + d[0]) % 8
     c = (w % 2 + d[1]) % 2
     return (w // 4) * 4 + (z % 2) * 2 + c, z // 2
+
+
+def same_core_peer(w, n, d):
+    w, n = plane_peer(w, n, d[:2])
+    return line_peer(w, n, (d[2], 0))
 
 
 def around_peer(w, n, d):
@@ -212,20 +220,19 @@
     raster_ref, trans_ref, kern_ref, weight_ref, lib_ref, tile_ref, corner_ref,
     aerial_ref, score_ref,
     mask, ext, raw_taps, perm, taps, spread, row_basis, col_basis, select,
-    lib_raw, units, slots, parts, sums, clips, runs, ring_lse, plane_lse,
+    lib_raw, units, slots, parts, sums, clips, turned, own_lse, all_lse,
     halo_send, halo_recv, lib_sem, pair_send, pair_recv,
     line_send, line_recv, sum_send, sum_recv, all_send, all_recv,
-    ring_send, ring_recv, plane_send, plane_recv,
+    lse_send, lse_recv,
 ):
     w, n = place()
     g = w // 4
     core = w % 2
     line_me = (w % 4) * 4 + n
-    z_me = n * 2 + (w // 2) % 2
+    me = g * 8 + n * 2 + (w // 2) % 2
     around = [around_peer(w, n, d) for d in AROUND]
     line = [line_peer(w, n, d) for d in LINE]
     plane = [plane_peer(w, n, d) for d in PLANE]
-    ring = [line_peer(w, n, (d, 0)) for d in RING]
 
     barrier = pltpu.get_barrier_semaphore()
     peers = around + line + plane
@@ -340,57 +347,39 @@
     wait_bytes(clips.at[0:15], all_recv)
 
     scale = SHARP * math.log2(math.e)
-    for half in range(2):
-        chosen = clips[half * 8 : half * 8 + 8].reshape(256, SIGD)
-        runs[0] = jnp.full((8, 256), -4.0, F32)
-        runs[1] = jnp.zeros((8, 256), F32)
-        for source in range(2):
-
-            def match(i, carry):
-                block = units[source, pl.ds(pl.multiple_of(i * 512, 512), 512), :]
-                near = dot_nt(block, chosen).reshape(64, 8, 256)
-                old = runs[0]
-                top = jnp.maximum(old, jnp.max(near, axis=0))
-                gain = jnp.sum(jnp.exp2((near - top[None]) * scale), axis=0)
-                runs[1] = runs[1] * jnp.exp2((old - top) * scale) + gain
-                runs[0] = top
-                return carry
-
-            lax.fori_loop(0, LIB_DEV // 512, match, 0)
-        tops = runs[0]
-        top = jnp.max(tops, axis=0, keepdims=True)
-        weighted = runs[1] * jnp.exp2((tops - top) * scale)
-        amount = jnp.sum(weighted, axis=0, keepdims=True)
-        ring_lse[z_me, :, half * 256 : half * 256 + 256] = (top - 1.0) * SHARP + jnp.log(amount)
-
-    def joined(parts_ref, count):
-        values = [parts_ref[i] for i in range(count)]
-        top = values[0]
-        for v in values[1:]:
-            top = jnp.maximum(top, v)
-        amount = jnp.exp(values[0] - top)
-        for v in values[1:]:
-            amount += jnp.exp(v - top)
-        return top + jnp.log(amount)
-
-    for peer in ring:
-        send(ring_lse.at[z_me], ring_lse.at[z_me], ring_send, ring_recv, peer)
-    wait_bytes(ring_lse.at[0:7], ring_recv)
-    plane_lse[g] = joined(ring_lse, 8)
-    for peer in plane:
-        send(plane_lse.at[g], plane_lse.at[g], plane_send, plane_recv, peer)
-    wait_bytes(plane_lse.at[0:15], plane_recv)
-    score = joined(plane_lse, GROUPS) / (-SHARP)
-    first = g * 32 + ((w // 2) % 2) * 16 + n * 4
-    spot = iota((1, OWN_IDS), 1)
+    turned[...] = jnp.transpose(clips[...].reshape(OWN_IDS, SIGD))
+    tops = jnp.full((8, OWN_IDS), -4.0, F32)
+    sums_of = jnp.zeros((8, OWN_IDS), F32)
+    for block in range(2 * LIB_DEV // 512):
+        at = (block % 4) * 512
+        near = dot(units[block // 4, at : at + 512, :], turned[...]).reshape(64, 8, OWN_IDS)
+        old = tops
+        tops = jnp.maximum(old, jnp.max(near, axis=0))
+        gain = jnp.sum(jnp.exp2((near - tops[None]) * scale), axis=0)
+        sums_of = sums_of * jnp.exp2((old - tops) * scale) + gain
+    top = jnp.max(tops, axis=0, keepdims=True)
+    amount = jnp.sum(sums_of * jnp.exp2((tops - top) * scale), axis=0, keepdims=True)
+    found = (top - 1.0) * SHARP + jnp.log(amount)
+    for block in range(4):
+        own_lse[block] = found[:, block * 128 : block * 128 + 128]
+
+    for d in SAME_CORE:
+        peer = same_core_peer(w, n, d)
+        send(own_lse.at[peer[0] // 16], all_lse.at[me], lse_send, lse_recv, peer)
+    all_lse[me] = own_lse[g // 4]
+    wait_bytes(all_lse.at[0:127], lse_recv)
+    every = all_lse[...]
+    top = jnp.max(every, axis=0)
+    score = (top + jnp.log(jnp.sum(jnp.exp(every - top[None]), axis=0))) / (-SHARP)
+    first = (g % 4) * 32 + ((w // 2) % 2) * 16 + n * 4
+    spot = iota((1, 128), 1)
     for t in range(4):
         score_ref[t] = jnp.sum(jnp.where(spot == first + t, score, 0.0))
 
     wait_bytes(slots.at[0:15], line_send)
     wait_bytes(sums.at[0:15], sum_send)
     wait_bytes(clips.at[0:15], all_send)
-    wait_bytes(ring_lse.at[0:7], ring_send)
-    wait_bytes(plane_lse.at[0:15], plane_send)
+    wait_bytes(all_lse.at[0:127], lse_send)
 
 
 def per_device(raster, transmission, kernels, kernel_weight, library, clip_tile, clip_corner):
@@ -421,11 +410,11 @@
             pltpu.VMEM((GROUPS, 32, SIGD), BF16),
             pltpu.VMEM((GROUPS, 32, SIGD), BF16),
             pltpu.VMEM((GROUPS, 32, SIGD), BF16),
-            pltpu.VMEM((2, 8, 256), F32),
-            pltpu.VMEM((8, 1, OWN_IDS), F32),
-            pltpu.VMEM((GROUPS, 1, OWN_IDS), F32),
+            pltpu.VMEM((SIGD, OWN_IDS), BF16),
+            pltpu.VMEM((4, 1, 128), F32),
+            pltpu.VMEM((128, 1, 128), F32),
             dma((8,)), dma((8,)), dma, dma, dma,
-            dma, dma, dma, dma, dma, dma, dma, dma, dma, dma,
+            dma, dma, dma, dma, dma, dma, dma, dma,
         ],
         compiler_params=pltpu.CompilerParams(
             collective_id=0, has_side_effects=True, vmem_limit_bytes=56 * 1024 * 1024

time: 61.1 us -> 55.6 us (0.910)
  Pallas kernels: 58.2 us -> 52.8 us
    pallas_call x1, Pallas kernels: 58.2 us -> 52.8 us  [per_device(): pl.pallas_call(kernel, out_shape=(jax.ShapeDtypeStruct((TILE, TILE), F32)...]
where the time goes in v2:
time: 55.6 us; the launch traced here: 55.4 us
  Pallas kernels  52.8 us (95%)
  local copies, waits for them, and re-layouts  1.99 us (4%)
  between operations  0.65 us (1%)
    pallas_call x1, Pallas kernels, per_device(): pl.pallas_call(kernel, out_shape=(jax.ShapeDtypeStruct((TILE, TILE), F32)...  52.8 us
    unnamed x4, local copies, waits for them, and re-layouts  1.99 us

profile of v2, /device:TPU:32, one launch (start us, length us, event | category | flops | bytes accessed | tf_op | source)
XLA Modules:
  0.0 55.4 jit_solution(12854199303023206206)
XLA Ops:
  0.6 52.8 %shard_map.86 = (f32[128,128]{1,0:T(8,128)}, f32[4]{0:T(128)}) custom-call(s32[128,128]{1,0:T(8,128)} %raster_ref.1, bf16[128,128]{1,0:T(8,128)(2,1)} %trans_ref.1, f32[1024,64]{1,0:T(8,128)} %bitcast.2, f32[8]{0:T(128)} %weight_ref.1, bf16[2048,256]{1,0:T(8,128)(2,1)} %lib_ref.1, s32[8,128]{1,0:T(8,128)} %bitcast.3, s32[2,1024]{1,0:T(2,128)} %corner_ref.1), custom_call_target="tpu_custom_call" | custom-call | tf_op jit(solution)/shard_map/pallas_call | solution.py:389
  53.4 0.0 copy-start
  53.5 1.5 %copy.11 = f32[128,128]{1,0:T(8,128)} copy(f32[128,128]{1,0:T(8,128)} %get-tuple-element.4) | data formatting | bytes 131072
  54.9 0.0 copy-done
  54.9 0.5 copy.12
Async XLA Ops:
  53.4 1.5 %copy-start = (f32[4]{0:T(128)S(1)}, f32[4]{0:T(128)}, u32[]{:S(2)}) copy-start(f32[4]{0:T(128)} %get-tuple-element.5) | copy-start | bytes 52

commit v3 on v2

--- a/solution.py
+++ b/solution.py
@@ -39,7 +39,7 @@
     [(dx, dy, dz) for dx in range(4) for dy in range(4) for dz in range(8) if dx or dy or dz],
     key=lambda d: -(min(d[0], 4 - d[0]) + min(d[1], 4 - d[1]) + min(d[2], 8 - d[2])),
 )
-AROUND = [(dw, dn) for dw in (1, -1, 0) for dn in (1, -1, 0) if dw or dn]
+AROUND = [(1, 0), (-1, 0), (0, 1), (0, -1)]
 
 
 def place():
@@ -196,32 +196,41 @@
         select[r * 64 : r * 64 + 64, :] = (key == slot_key).astype(F32).astype(BF16)
 
 
-def shifted_copies(ext, spread):
-    lane = iota((192, 128), 1)
-    left = pltpu.roll(ext[0], HALF, 1)
-    mid = pltpu.roll(ext[1], HALF, 1)
-    right = pltpu.roll(ext[2], HALF, 1)
+def shifted_copies(left, mid, right, places):
+    lane = iota(mid.shape, 1)
+    mid = pltpu.roll(mid, HALF, 1)
     low = jnp.where(lane < HALF, left, mid)
     high = jnp.where(lane < HALF, mid, right)
     for j in range(TAPS):
         moved = jnp.where(lane < j, high, low)
         if j:
             moved = pltpu.roll(moved, 128 - j, 1)
-        for rb in range(12):
-            block = moved[rb * 16 : rb * 16 + 16]
-            if rb < 8:
-                spread[rb * 1024 + j * 16 : rb * 1024 + j * 16 + 16, 0:128] = block
-            if rb >= 4:
-                at = (rb - 4) * 1024 + j * 16
-                spread[at : at + 16, 128:256] = block
+        for b, where in enumerate(places):
+            for ref, index, at in where:
+                row = index * 1024 + j * 16
+                ref[row : row + 16, at : at + 128] = moved[b * 16 : b * 16 + 16]
+
+
+def rolled(x, shift):
+    return pltpu.roll(x, shift % 128, 1) if shift % 128 else x
+
+
+def pack_side(mask, first):
+    lane = iota((HALF, TILE), 1)
+    packed = jnp.zeros((HALF, TILE), BF16)
+    for q in range(4):
+        moved = rolled(mask[q * 32 : q * 32 + 32, :], q * 32 - first)
+        packed = jnp.where(lane // 32 == q, moved, packed)
+    return packed
 
 
 def kernel(
-    raster_ref, trans_ref, kern_ref, weight_ref, lib_ref, tile_ref, corner_ref,
+    raster_hbm, trans_hbm, kern_hbm, weight_hbm, lib_ref, tile_hbm, corner_hbm,
     aerial_ref, score_ref,
-    mask, ext, raw_taps, perm, taps, spread, row_basis, col_basis, select,
+    raster_ref, trans_ref, kern_ref, weight_ref, tile_ref, corner_ref, in_sem,
+    mask, packed, side, edge, corner, raw_taps, perm, taps, inner, outer, row_basis, col_basis, select,
     lib_raw, units, slots, parts, sums, clips, turned, own_lse, all_lse,
-    halo_send, halo_recv, lib_sem, pair_send, pair_recv,
+    halo_send, halo_recv, corner_send, corner_recv, lib_sem, pair_send, pair_recv,
     line_send, line_recv, sum_send, sum_recv, all_send, all_recv,
     lse_send, lse_recv,
 ):
@@ -238,10 +247,22 @@
     peers = around + line + plane
     for peer in peers:
         pl.semaphore_signal(barrier, inc=1, device_id=peer, device_id_type=MESH)
+    inputs = [
+        pltpu.make_async_copy(src, dst, in_sem.at[i])
+        for i, (src, dst) in enumerate([
+            (raster_hbm, raster_ref), (trans_hbm, trans_ref), (kern_hbm, kern_ref),
+            (weight_hbm, weight_ref), (tile_hbm, tile_ref), (corner_hbm, corner_ref),
+        ])
+    ]
+    for copy in inputs:
+        copy.start()
     lib_copy = pltpu.make_async_copy(lib_ref, lib_raw, lib_sem)
     lib_copy.start()
+    for copy in inputs:
+        copy.wait()
     mask[...] = (raster_ref[...].astype(F32) * trans_ref[...].astype(F32)).astype(BF16)
-    ext[1, HALF : HALF + TILE, :] = mask[...]
+    packed[0] = pack_side(mask[...], 0)
+    packed[1] = pack_side(mask[...], 96)
     build_taps(kern_ref, raw_taps, perm, taps)
     pl.semaphore_wait(barrier, len(peers))
 
@@ -254,10 +275,8 @@
         return copy
 
     halo = []
-    for i, (dw, dn) in enumerate(AROUND):
-        src = {0: mask, 1: mask.at[TILE - HALF : TILE], -1: mask.at[0:HALF]}[dn]
-        to = {0: slice(HALF, HALF + TILE), 1: slice(0, HALF), -1: slice(HALF + TILE, 2 * HALF + TILE)}[dn]
-        dst = ext.at[1 - dw, to]
+    pieces = [(packed.at[1], side.at[0]), (packed.at[0], side.at[1]), (mask.at[96:128], edge.at[0]), (mask.at[0:32], edge.at[1])]
+    for i, (src, dst) in enumerate(pieces):
         halo.append(send(src, dst, halo_send.at[i], halo_recv.at[i], around[i]))
 
     lib_copy.wait()
@@ -273,46 +292,76 @@
     own_bases(w, n, tile_ref, corner_ref, row_basis, col_basis)
     build_select(w, tile_ref, select)
 
-    for copy in halo:
+    for copy in halo[:2]:
         copy.wait()
-    zero_side = jnp.zeros((192, TILE), BF16)
-    zero_rows = jnp.zeros((3, HALF, TILE), BF16)
 
     @pl.when(w == 0)
     def _():
-        ext[0] = zero_side
+        side[0] = jnp.zeros((HALF, TILE), BF16)
 
     @pl.when(w == 63)
     def _():
-        ext[2] = zero_side
-
-    @pl.when(n == 0)
-    def _():
-        ext[:, 0:HALF, :] = zero_rows
-
-    @pl.when(n == 3)
-    def _():
-        ext[:, HALF + TILE : 2 * HALF + TILE, :] = zero_rows
-
-    shifted_copies(ext, spread)
+        side[1] = jnp.zeros((HALF, TILE), BF16)
+
+    below, above = around[2], around[3]
+    pieces = [(side, corner.at[0], below), (side, corner.at[1], above)]
+    corners = []
+    for i, (src, dst, peer) in enumerate(pieces):
+        corners.append(send(src, dst, corner_send.at[i], corner_recv.at[i], peer))
+
+    places = [[] for _ in range(8)]
+    for b in range(8):
+        rb = b + 2
+        if rb < 8:
+            places[b].append((inner, rb - 2, 0))
+        if rb >= 4:
+            places[b].append((inner, rb - 4, 128))
+        places[b].append((outer, rb, 0) if rb < 6 else (outer, rb - 6, 128))
+    lefts = jnp.concatenate([rolled(side[0], -32 * q) for q in range(4)], axis=0)
+    rights = jnp.concatenate([rolled(side[1], 32 - 32 * q) for q in range(4)], axis=0)
+    shifted_copies(lefts, mask[...], rights, places)
 
     field_index = iota((16, 256), 0) // 2
     weight = jnp.zeros((16, 256), F32)
     for k in range(8):
         weight = jnp.where(field_index == k, weight_ref[k], weight)
 
-    def rows(i, carry):
-        window = spread[pl.ds(pl.multiple_of(i * 1024, 1024), DEPTH), :]
-        both = dot(taps[...], window)
-        field = both[0:256] + both[256:512]
-        energy = (field * field).reshape(SHIFTS, FIELDS, 256) * weight[None]
-        image = jnp.sum(energy, axis=1)
-        at = pl.multiple_of(i * 16, 16)
-        aerial_ref[pl.ds(at, 16), :] = image[:, 0:128]
-        aerial_ref[pl.ds(at + 64, 16), :] = image[:, 128:256]
-        return carry
-
-    lax.fori_loop(0, 4, rows, 0)
+    def rows(source, first, second):
+        def pair_of_blocks(i, carry):
+            window = source[pl.ds(pl.multiple_of(i * 1024, 1024), DEPTH), :]
+            both = dot(taps[...], window)
+            field = both[0:256] + both[256:512]
+            energy = (field * field).reshape(SHIFTS, FIELDS, 256) * weight[None]
+            image = jnp.sum(energy, axis=1)
+            at = pl.multiple_of(i * 16, 16)
+            aerial_ref[pl.ds(at + first * 16, 16), :] = image[:, 0:128]
+            aerial_ref[pl.ds(at + second * 16, 16), :] = image[:, 128:256]
+            return carry
+
+        lax.fori_loop(0, 2, pair_of_blocks, 0)
+
+    rows(inner, 2, 4)
+    for copy in halo[2:] + corners:
+        copy.wait()
+
+    @pl.when(n == 0)
+    def _():
+        edge[0] = jnp.zeros((HALF, TILE), BF16)
+        corner[0] = jnp.zeros((2, HALF, TILE), BF16)
+
+    @pl.when(n == 3)
+    def _():
+        edge[1] = jnp.zeros((HALF, TILE), BF16)
+        corner[1] = jnp.zeros((2, HALF, TILE), BF16)
+
+    places = [[(outer, 0, 0)], [(outer, 1, 0)], [(outer, 4, 128)], [(outer, 5, 128)]]
+    shifted_copies(
+        jnp.concatenate([rolled(corner[0, 0], -96), corner[1, 0]], axis=0),
+        edge[...].reshape(2 * HALF, TILE),
+        jnp.concatenate([rolled(corner[0, 1], -64), rolled(corner[1, 1], 32)], axis=0),
+        places,
+    )
+    rows(outer, 0, 6)
 
     halfway = dot(row_basis[...], aerial_ref[...], HIGHEST)
     cross = dot_nt(halfway, col_basis[...], HIGHEST)
@@ -383,24 +432,32 @@
 
 
 def per_device(raster, transmission, kernels, kernel_weight, library, clip_tile, clip_corner):
-    vmem = pl.BlockSpec(memory_space=pltpu.VMEM)
+    hbm = pl.BlockSpec(memory_space=pl.ANY)
     smem = pl.BlockSpec(memory_space=pltpu.SMEM)
     dma = pltpu.SemaphoreType.DMA
     return pl.pallas_call(
         kernel,
-        out_shape=(
-            jax.ShapeDtypeStruct((TILE, TILE), F32),
-            jax.ShapeDtypeStruct((4,), F32),
-        ),
-        in_specs=[vmem, vmem, vmem, smem, pl.BlockSpec(memory_space=pl.ANY), vmem, vmem],
-        out_specs=(vmem, smem),
+        out_shape=(pltpu.VMEM((TILE, TILE), F32), jax.ShapeDtypeStruct((4,), F32)),
+        in_specs=[hbm] * 7,
+        out_specs=(pl.BlockSpec(memory_space=pltpu.VMEM), smem),
         scratch_shapes=[
+            pltpu.VMEM((TILE, TILE), I32),
             pltpu.VMEM((TILE, TILE), BF16),
-            pltpu.VMEM((3, 192, TILE), BF16),
+            pltpu.VMEM((FIELDS * TAPS, TAPS), F32),
+            pltpu.SMEM((8,), F32),
+            pltpu.VMEM((8, 128), I32),
+            pltpu.VMEM((2, CLIPS), I32),
+            dma((6,)),
+            pltpu.VMEM((TILE, TILE), BF16),
+            pltpu.VMEM((2, HALF, TILE), BF16),
+            pltpu.VMEM((2, HALF, TILE), BF16),
+            pltpu.VMEM((2, HALF, TILE), BF16),
+            pltpu.VMEM((2, 2, HALF, TILE), BF16),
             pltpu.VMEM((128, 1024), BF16),
             pltpu.VMEM((1024, 1024), BF16),
             pltpu.VMEM((512, DEPTH), BF16),
-            pltpu.VMEM((8 * 1024, 256), BF16),
+            pltpu.VMEM((6 * 1024, 256), BF16),
+            pltpu.VMEM((6 * 1024, 256), BF16),
             pltpu.VMEM((256, TILE), F32),
             pltpu.VMEM((256, TILE), F32),
             pltpu.VMEM((OWN_IDS, 256), BF16),
@@ -413,7 +470,7 @@
             pltpu.VMEM((SIGD, OWN_IDS), BF16),
             pltpu.VMEM((4, 1, 128), F32),
             pltpu.VMEM((128, 1, 128), F32),
-            dma((8,)), dma((8,)), dma, dma, dma,
+            dma((4,)), dma((4,)), dma((2,)), dma((2,)), dma, dma, dma,
             dma, dma, dma, dma, dma, dma, dma, dma,
         ],
         compiler_params=pltpu.CompilerParams(

time: 55.6 us -> 53.2 us (0.957)
  Pallas kernels: 52.8 us -> 51.3 us
  local copies, waits for them, and re-layouts: 1.99 us -> 1.15 us
    pallas_call x1, Pallas kernels: 52.8 us -> 51.3 us  [per_device(): pl.pallas_call(kernel, out_shape=(pltpu.VMEM((TILE, TILE), F32), jax.Shap...]
    unnamed x4, local copies, waits for them, and re-layouts: 1.99 us -> 1.15 us
where the time goes in v3:
time: 53.2 us; the launch traced here: 53.1 us
  Pallas kernels  51.3 us (96%)
  local copies, waits for them, and re-layouts  1.15 us (2%)
  between operations  0.65 us (1%)
    pallas_call x1, Pallas kernels, per_device(): pl.pallas_call(kernel, out_shape=(pltpu.VMEM((TILE, TILE), F32), jax.Shap...  51.3 us
    unnamed x4, local copies, waits for them, and re-layouts  1.15 us

profile of v3, /device:TPU:32, one launch (start us, length us, event | category | flops | bytes accessed | tf_op | source)
XLA Modules:
  0.0 53.1 jit_solution(16623134141176214729)
XLA Ops:
  0.6 51.3 %shard_map.86 = (f32[128,128]{1,0:T(8,128)S(1)}, f32[4]{0:T(128)}) custom-call(s32[128,128]{1,0:T(8,128)} %raster_hbm.1, bf16[128,128]{1,0:T(8,128)(2,1)} %trans_hbm.1, f32[1024,64]{1,0:T(8,128)} %bitcast.2, f32[8]{0:T(128)} %weight_hbm.1, bf16[2048,256]{1,0:T(8,128)(2,1)} %lib_ref.1, s32[8,128]{1,0:T(8,128)} %bitcast.3, s32[2,1024]{1,0:T(2,128)} %corner_hbm.1), custom_call_target="tpu_custom_call" | custom-call | tf_op jit(solution)/shard_map/pallas_call | solution.py:438
  52.0 0.0 copy-start
  52.0 0.6 %copy.11 = f32[128,128]{1,0:T(8,128)} copy(f32[128,128]{1,0:T(8,128)S(1)} %get-tuple-element.2) | data formatting | bytes 131072
  52.6 0.0 copy-done
  52.6 0.5 copy.12
Async XLA Ops:
  52.0 0.6 %copy-start = (f32[4]{0:T(128)S(1)}, f32[4]{0:T(128)}, u32[]{:S(2)}) copy-start(f32[4]{0:T(128)} %get-tuple-element.7) | copy-start | bytes 52

commit v4 on v3

--- a/solution.py
+++ b/solution.py
@@ -59,11 +59,6 @@
     z = (n * 2 + (w // 2) % 2 + d[0]) % 8
     c = (w % 2 + d[1]) % 2
     return (w // 4) * 4 + (z % 2) * 2 + c, z // 2
-
-
-def same_core_peer(w, n, d):
-    w, n = plane_peer(w, n, d[:2])
-    return line_peer(w, n, (d[2], 0))
 
 
 def around_peer(w, n, d):
@@ -327,18 +322,17 @@
         weight = jnp.where(field_index == k, weight_ref[k], weight)
 
     def rows(source, first, second):
-        def pair_of_blocks(i, carry):
-            window = source[pl.ds(pl.multiple_of(i * 1024, 1024), DEPTH), :]
+        def pair_of_blocks(i):
+            window = source[i * 1024 : i * 1024 + DEPTH, :]
             both = dot(taps[...], window)
             field = both[0:256] + both[256:512]
             energy = (field * field).reshape(SHIFTS, FIELDS, 256) * weight[None]
             image = jnp.sum(energy, axis=1)
-            at = pl.multiple_of(i * 16, 16)
-            aerial_ref[pl.ds(at + first * 16, 16), :] = image[:, 0:128]
-            aerial_ref[pl.ds(at + second * 16, 16), :] = image[:, 128:256]
-            return carry
-
-        lax.fori_loop(0, 2, pair_of_blocks, 0)
+            for lane, block in ((0, first + i), (128, second + i)):
+                aerial_ref[block * 16 : block * 16 + 16, :] = image[:, lane : lane + 128]
+
+        for i in range(2):
+            pair_of_blocks(i)
 
     rows(inner, 2, 4)
     for copy in halo[2:] + corners:
@@ -412,9 +406,14 @@
     for block in range(4):
         own_lse[block] = found[:, block * 128 : block * 128 + 128]
 
-    for d in SAME_CORE:
-        peer = same_core_peer(w, n, d)
-        send(own_lse.at[peer[0] // 16], all_lse.at[me], lse_send, lse_recv, peer)
+    columns = {(0, 0): g} | {d: plane[i][0] // 4 for i, d in enumerate(PLANE)}
+    quarters = {d: c // 4 for d, c in columns.items()}
+    starts = {d: c * 4 for d, c in columns.items()}
+    rows_z = {d: line_peer(w, n, (d, 0)) for d in range(8)}
+    within = {d: p[0] % 4 for d, p in rows_z.items()}
+    for dx, dy, dz in SAME_CORE:
+        peer = (starts[dx, dy] + within[dz], rows_z[dz][1])
+        send(own_lse.at[quarters[dx, dy]], all_lse.at[me], lse_send, lse_recv, peer)
     all_lse[me] = own_lse[g // 4]
     wait_bytes(all_lse.at[0:127], lse_recv)
     every = all_lse[...]

time: 53.2 us -> 52.6 us (0.989)
  Pallas kernels: 51.3 us -> 50.7 us
    pallas_call x1, Pallas kernels: 51.3 us -> 50.7 us  [per_device(): pl.pallas_call(kernel, out_shape=(pltpu.VMEM((TILE, TILE), F32), jax.Shap...]
where the time goes in v4:
time: 52.6 us; the launch traced here: 52.5 us
  Pallas kernels  50.7 us (96%)
  local copies, waits for them, and re-layouts  1.15 us (2%)
  between operations  0.65 us (1%)
    pallas_call x1, Pallas kernels, per_device(): pl.pallas_call(kernel, out_shape=(pltpu.VMEM((TILE, TILE), F32), jax.Shap...  50.7 us
    unnamed x4, local copies, waits for them, and re-layouts  1.15 us

profile of v4, /device:TPU:32, one launch (start us, length us, event | category | flops | bytes accessed | tf_op | source)
XLA Modules:
  0.0 52.5 jit_solution(6688043510936088841)
XLA Ops:
  0.6 50.7 %shard_map.86 = (f32[128,128]{1,0:T(8,128)S(1)}, f32[4]{0:T(128)}) custom-call(s32[128,128]{1,0:T(8,128)} %raster_hbm.1, bf16[128,128]{1,0:T(8,128)(2,1)} %trans_hbm.1, f32[1024,64]{1,0:T(8,128)} %bitcast.2, f32[8]{0:T(128)} %weight_hbm.1, bf16[2048,256]{1,0:T(8,128)(2,1)} %lib_ref.1, s32[8,128]{1,0:T(8,128)} %bitcast.3, s32[2,1024]{1,0:T(2,128)} %corner_hbm.1), custom_call_target="tpu_custom_call" | custom-call | tf_op jit(solution)/shard_map/pallas_call | solution.py:437
  51.3 0.0 copy-start
  51.4 0.6 %copy.11 = f32[128,128]{1,0:T(8,128)} copy(f32[128,128]{1,0:T(8,128)S(1)} %get-tuple-element.2) | data formatting | bytes 131072
  52.0 0.0 copy-done
  52.0 0.5 copy.12
Async XLA Ops:
  51.3 0.6 %copy-start = (f32[4]{0:T(128)S(1)}, f32[4]{0:T(128)}, u32[]{:S(2)}) copy-start(f32[4]{0:T(128)} %get-tuple-element.7) | copy-start | bytes 52

commit v5 on v4

--- a/solution.py
+++ b/solution.py
@@ -362,8 +362,11 @@
     row = iota((256, 256), 0)
     lane = iota((256, 256), 1)
     cross = jnp.where(row // 16 == lane // 16, cross, 0.0)
-    fold = (row % 16 == lane % 16).astype(F32)
-    wide = jnp.where(row % 16 == lane // 16, dot(cross, fold, HIGHEST), 0.0)
+    folded = cross[:, 0:128] + cross[:, 128:256]
+    for shift in (64, 32, 16):
+        folded = folded + pltpu.roll(folded, shift, 1)
+    folded = jnp.concatenate([folded, folded], axis=1)
+    wide = jnp.where(row % 16 == lane // 16, folded, 0.0)
     signature = jnp.sum(wide.reshape(CAP, KSIG, SIGD), axis=1)
     signature = jnp.where(iota((CAP, SIGD), 1) == 0, 0.0, signature)
     slots[line_me] = unit_rows(signature)

time: 52.6 us -> 52.3 us (level)
  no operation moved by 1% of the time
where the time goes in v5:
time: 52.3 us; the launch traced here: 52.2 us
  Pallas kernels  50.4 us (96%)
  local copies, waits for them, and re-layouts  1.15 us (2%)
  between operations  0.65 us (1%)
    pallas_call x1, Pallas kernels, per_device(): pl.pallas_call(kernel, out_shape=(pltpu.VMEM((TILE, TILE), F32), jax.Shap...  50.4 us
    unnamed x4, local copies, waits for them, and re-layouts  1.15 us

profile of v5, /device:TPU:32, one launch (start us, length us, event | category | flops | bytes accessed | tf_op | source)
XLA Modules:
  0.0 52.2 jit_solution(15719130793519021128)
XLA Ops:
  0.6 50.4 %shard_map.86 = (f32[128,128]{1,0:T(8,128)S(1)}, f32[4]{0:T(128)}) custom-call(s32[128,128]{1,0:T(8,128)} %raster_hbm.1, bf16[128,128]{1,0:T(8,128)(2,1)} %trans_hbm.1, f32[1024,64]{1,0:T(8,128)} %bitcast.2, f32[8]{0:T(128)} %weight_hbm.1, bf16[2048,256]{1,0:T(8,128)(2,1)} %lib_ref.1, s32[8,128]{1,0:T(8,128)} %bitcast.3, s32[2,1024]{1,0:T(2,128)} %corner_hbm.1), custom_call_target="tpu_custom_call" | custom-call | tf_op jit(solution)/shard_map/pallas_call | solution.py:440
  51.1 0.0 copy-start
  51.1 0.6 %copy.11 = f32[128,128]{1,0:T(8,128)} copy(f32[128,128]{1,0:T(8,128)S(1)} %get-tuple-element.2) | data formatting | bytes 131072
  51.7 0.0 copy-done
  51.7 0.5 copy.12
Async XLA Ops:
  51.1 0.6 %copy-start = (f32[4]{0:T(128)S(1)}, f32[4]{0:T(128)}, u32[]{:S(2)}) copy-start(f32[4]{0:T(128)} %get-tuple-element.7) | copy-start | bytes 52
